TPU v7x, 256 devices: a whole 4x4x8 slice. The times are simulated.
256 devices in a mesh: src: 8 (over y, core), tgt: 32 (over x, z).
Axes of the slice: x: 4, y: 4, z: 8, core: 2. Of those that a mesh axis runs over, the one named last changes fastest.
Arguments:
- source_features: bfloat16 [8192, 128], P('src'), may hold values from -20 to 20
- target_features: bfloat16 [32768, 128], P('tgt'), may hold values from -20 to 20
- source_logmass: float32 [8192], P('src'), may hold values from -1 to 1
- target_logmass: float32 [32768], P('tgt'), may hold values from -1 to 1
- teacher_rows: bfloat16 [32768, 1536], P('tgt'), may hold values from -6 to 6
Outputs:
- projected: bfloat16 [8192, 1536], P(('src', 'tgt'))
- source_potential: float32 [8192], P('src')
- target_potential: float32 [32768], P('tgt')
All inputs are finite; a program needn't handle non-finite values.
Results may differ from a plain program's by a relative error of at most 0.0049.
Values sent between devices are 32-bit elements; how exact they have to be, the bound alone decides.
A program may use at most 64 MiB of HBM per device.

v0:
```python
import functools
import math

import jax
import jax.numpy as jnp
from jax import lax
from jax.experimental import pallas as pl
from jax.experimental.pallas import tpu as pltpu
from jax.sharding import PartitionSpec as P

MESH = pl.DeviceIdType.MESH
EPS = 0.1
LOG2E = math.log2(math.e)
LN2 = math.log(2.0)
NX, NY, NZ = 4, 4, 8
LANES = 128
TILE = 1024
BLK = TILE // LANES
ROWS = 32
HALF = TILE // 2
NEAR = 4
CHUNKS = 12
KINDS = "ABABBAHHHHHH"
DIRECT = (1, 3, 5)
SCHEDULE = (
    ("s", 0), ("s", 1), ("ao", 0), ("bo", 1), ("s", 2), ("s", 3), ("qm", 0), ("s", 4), ("br", 1, 1, 0),
    ("br", 1, 1, 1), ("ao", 2), ("bo", 3), ("ap", 0, 0), ("ap", 0, 1), ("bo", 4), ("hw", 0), ("s", 6), ("hf", 0),
    ("br", 3, 1, 0), ("br", 3, 1, 1), ("s", 7), ("br", 4, 1, 0), ("ap", 2, 0), ("ap", 2, 1), ("br", 4, 1, 1),
    ("br", 1, 2, 0), ("br", 1, 2, 1), ("s", 8), ("s", 9), ("ht", 0), ("s", 10), ("br", 3, 2, 0), ("br", 3, 2, 1),
    ("am", 0), ("br", 4, 2, 0), ("br", 4, 2, 1), ("s", 11), ("br", 1, 3, 0), ("br", 1, 3, 1), ("hm", 7), ("hm", 6),
    ("br", 3, 3, 0), ("br", 3, 3, 1), ("ar", 0, 1, 0), ("ar", 0, 1, 1), ("am", 2), ("br", 4, 3, 0), ("br", 4, 3, 1),
    ("s", 5), ("ao", 5), ("bm", 1), ("ar", 7, 1, 0), ("ar", 7, 1, 1), ("ar", 6, 1, 0), ("ar", 6, 1, 1), ("hm", 8),
    ("hm", 9), ("bm", 3), ("ar", 0, 2, 0), ("ar", 0, 2, 1), ("ar", 2, 1, 0), ("ar", 2, 1, 1), ("hm", 11), ("hm", 10),
    ("bm", 4), ("ar", 7, 2, 0), ("ar", 7, 2, 1), ("ar", 6, 2, 0), ("ar", 6, 2, 1), ("ar", 8, 1, 0), ("ar", 8, 1, 1),
    ("ar", 9, 1, 0), ("ar", 9, 1, 1), ("ap", 5, 0), ("ar", 0, 3, 0), ("ar", 0, 3, 1), ("ap", 5, 1), ("ar", 2, 2, 0),
    ("ar", 2, 2, 1), ("ar", 11, 1, 0), ("ar", 11, 1, 1), ("ar", 10, 1, 0), ("ar", 10, 1, 1), ("qe", 0), ("be", 1),
    ("ar", 7, 3, 0), ("ar", 7, 3, 1), ("ar", 6, 3, 0), ("ar", 6, 3, 1), ("be", 3), ("ar", 8, 2, 0), ("ar", 8, 2, 1),
    ("ar", 9, 2, 0), ("ar", 9, 2, 1), ("be", 4), ("ae", 0), ("ar", 2, 3, 0), ("ar", 2, 3, 1), ("ar", 11, 2, 0),
    ("ar", 11, 2, 1), ("ar", 10, 2, 0), ("ar", 10, 2, 1), ("am", 5), ("ae", 7), ("ae", 6), ("ar", 8, 3, 0),
    ("ar", 8, 3, 1), ("ar", 9, 3, 0), ("ar", 9, 3, 1), ("ae", 2), ("ar", 11, 3, 0), ("ar", 11, 3, 1),
    ("ar", 10, 3, 0), ("ar", 10, 3, 1), ("ad", 5), ("ae", 8), ("ae", 9), ("ae", 11), ("ae", 10),
)
NA, NH = KINDS.count("A"), KINDS.count("H")


def chunks_of(kind):
    return [ch for ch in range(CHUNKS) if KINDS[ch] == kind]


def kernel(feat, xs_hbm, ys_hbm, slm_hbm, tlm_hbm, rows_hbm, out, f_out, g_out,
           xs, ys, slm, tlm, score, hcol, weights, teach, part, rbuf, cbuf, vec, tmp4, qbuf,
           xfar, xnear, asum, zfar, znear, bfar, bnear, bsum, bx, rcol,
           load_sem, in_sem, rs_sem, rr_sem, cs_sem, cr_sem, qs_sem, qr_sem,
           as_sem, ar_sem, zs_sem, zr_sem, bs_sem, br_sem, bxs_sem, bxr_sem,
           zall, stage, gath, pscore, pweights, pteach, kvec, hsend, hrecv,
           gs_sem, gr_sem, ds_sem, dr_sem, ys_sem, yr_sem, ks_sem, kr_sem, hs_sem, hr_sem):
    src = lax.axis_index("src")
    tgt = lax.axis_index("tgt")
    y, c = lax.div(src, 2), lax.rem(src, 2)
    x, z = lax.div(tgt, NZ), lax.rem(tgt, NZ)
    xi = [lax.rem(x + d, NX) for d in range(NX)]
    zi = [lax.rem(z + d, NZ) for d in range(NZ)]

    def at_tgt(dx, dz):
        return (src, xi[dx % NX] * NZ + zi[dz % NZ])

    def at_src(dy, dc):
        return (lax.rem(y + dy, NY) * 2 + lax.rem(c + dc, 2), tgt)

    def hops(d, n):
        return min(d, n - d)

    tgt_peers = sorted([(dx, dz) for dx in range(NX) for dz in range(NZ) if dx or dz],
                       key=lambda o: -hops(o[0], NX) - hops(o[1], NZ))
    src_peers = sorted([(dy, dc) for dy in range(NY) for dc in range(2) if dy or dc],
                       key=lambda o: -hops(o[0], NY) - 0.1 * o[1])

    loads = [pltpu.make_async_copy(a, b, in_sem.at[n]) for n, (a, b) in enumerate(
        ((ys_hbm, ys), (xs_hbm, xs), (slm_hbm, slm), (tlm_hbm, tlm)))]
    for copy in loads:
        copy.start()
    load = pltpu.make_async_copy(rows_hbm, teach, load_sem)
    load.start()
    barrier = pltpu.get_barrier_semaphore()
    for o in tgt_peers:
        pl.semaphore_signal(barrier, inc=1, device_id=at_tgt(*o), device_id_type=MESH)
    for o in src_peers:
        pl.semaphore_signal(barrier, inc=1, device_id=at_src(*o), device_id_type=MESH)

    def remote(a, b, ssem, rsem, dev):
        pltpu.make_async_remote_copy(src_ref=a, dst_ref=b, send_sem=ssem, recv_sem=rsem,
                                     device_id=dev, device_id_type=MESH).start()

    def arrive(ref, sem):
        pltpu.make_async_copy(ref, ref, sem).wait()

    def row_exchange(e, value, meanwhile=None):
        rbuf[e, tgt] = value
        for o in tgt_peers:
            remote(rbuf.at[e, tgt], rbuf.at[e, tgt], rs_sem.at[e], rr_sem.at[e], at_tgt(*o))
        if meanwhile is not None:
            meanwhile()
        arrive(rbuf.at[e, pl.ds(0, 31)], rr_sem.at[e])
        return rbuf[e]

    def col_exchange(e, value, meanwhile=None):
        cbuf[e, src] = value
        for o in src_peers:
            remote(cbuf.at[e, src], cbuf.at[e, src], cs_sem.at[e], cr_sem.at[e], at_src(*o))
        if meanwhile is not None:
            meanwhile()
        arrive(cbuf.at[e, pl.ds(0, 7)], cr_sem.at[e])
        return cbuf[e]

    def lse2(parts):
        peak = jnp.max(parts, axis=0)
        return peak + jnp.log(jnp.sum(jnp.exp2(parts - peak), axis=0)) * LOG2E

    def col_form(row):
        return jnp.broadcast_to(row, (LANES, LANES)).T

    side = 1 - 2 * lax.rem(x, 2)
    mate_x = [lax.rem(x + side + NX, NX), lax.rem(x - side + NX, NX)]
    mates = [(src, m * NZ + z) for m in mate_x]
    sibling = (y * 2 + 1 - c, tgt)
    mine = pl.ds(c * HALF, HALF)

    def shared(u):
        return u < 2 or u >= 2 + NEAR

    def gather_send(*units):
        for u in units:
            at = (u, y) if shared(u) else (u,)
            remote(stage.at[at], gath.at[(u, c) + at[1:]], gs_sem.at[u], gr_sem.at[u], mates[u % 2])

    def gather_spread(*units):
        for u in units:
            arrive(gath.at[u, 0, 0], gr_sem.at[u])
            for d in (2, 1, 3):
                remote(gath.at[u, c, y], gath.at[u, c, y], ys_sem.at[u], yr_sem.at[u], at_src(d, 0))

    def gather_share(*units):
        for u in units:
            if shared(u):
                arrive(gath.at[u, 0, pl.ds(0, 3)], yr_sem.at[u])
            else:
                arrive(gath.at[u, 0], gr_sem.at[u])
            remote(gath.at[u, c], gath.at[u, c], ds_sem.at[u], dr_sem.at[u], sibling)

    def gather_end(u):
        arrive(gath.at[u, 0], dr_sem.at[u])

    def lanes(k):
        return slice(k * LANES, (k + 1) * LANES)

    def fold(t):
        return t.reshape(LANES // 8, 8, LANES)

    for copy in loads:
        copy.wait()
    slm2 = slm[...] * LOG2E
    tlm2 = tlm[...] * LOG2E
    norm_scale = LOG2E / (feat * EPS)
    for a in range(BLK):
        xf = xs[pl.ds(a * LANES, LANES), :].astype(jnp.float32)
        yf = ys[pl.ds(a * LANES, LANES), :].astype(jnp.float32)
        vec[0, pl.ds(a, 1), :] = jnp.sum((xf * xf).T, axis=0, keepdims=True)
        vec[1, pl.ds(a, 1), :] = jnp.sum((yf * yf).T, axis=0, keepdims=True)
    nx2 = vec[0] * norm_scale
    ny2 = vec[1] * norm_scale
    bias = tlm2 - ny2

    for a in range(BLK):
        d = lax.dot_general(xs[pl.ds(a * LANES, LANES), :], ys[...], (((1,), (1,)), ((), ())),
                            preferred_element_type=jnp.float32)
        e = d * (2.0 * norm_scale)
        score[a] = e
        t = [e[:, lanes(k)] + bias[k:k + 1, :] for k in range(BLK)]
        m = functools.reduce(jnp.maximum, t)
        m = jnp.max(m, axis=1, keepdims=True)
        s = functools.reduce(jnp.add, [jnp.exp2(v - m) for v in t])
        s = jnp.sum(s, axis=1, keepdims=True)
        lse = m + jnp.log(s) * LOG2E
        vec[2, pl.ds(a, 1), :] = jnp.broadcast_to(lse, (LANES, LANES)).T[0:1, :]
    stage[0] = ys[mine, :].astype(jnp.float32).reshape(4, LANES, LANES)
    stage[1] = stage[0]
    load.wait()
    for n, ch in enumerate(chunks_of("H")):
        stage[2 + n] = teach[mine, lanes(ch)].astype(jnp.float32).reshape(4, LANES, LANES)
    pl.semaphore_wait(barrier, len(tgt_peers) + len(src_peers))
    row2 = lse2(row_exchange(0, vec[2]))
    vec[6] = row2
    gather_send(0, 1, 2, 3)

    h = slm2 - row2
    peaks = [jnp.full((8, LANES), -jnp.inf, jnp.float32)] * BLK
    for a in range(BLK):
        hc = col_form(h[a:a + 1, :])
        hcol[a] = hc
        for k in range(BLK):
            peaks[k] = jnp.maximum(peaks[k], jnp.max(fold(score[a, :, lanes(k)] + hc), axis=0))
    peaks = [jnp.max(p, axis=0, keepdims=True) for p in peaks]
    sums = [jnp.zeros((8, LANES), jnp.float32)] * BLK
    for a in range(BLK):
        hc = hcol[a]
        for k in range(BLK):
            sums[k] = sums[k] + jnp.sum(fold(jnp.exp2(score[a, :, lanes(k)] + hc - peaks[k])), axis=0)
    for k in range(BLK):
        total = jnp.sum(sums[k], axis=0, keepdims=True)
        vec[3, pl.ds(k, 1), :] = peaks[k] + jnp.log(total) * LOG2E
    col2 = lse2(col_exchange(0, vec[3]))
    gather_spread(0, 1)

    tmass = jnp.exp(tlm[...])
    smass = jnp.exp(slm[...])
    for a in range(BLK):
        lc = col_form(row2[a:a + 1, :])
        acc = None
        for k in range(BLK):
            q = jnp.exp2(score[a, :, lanes(k)] - lc - col2[k:k + 1, :])
            score[a, :, lanes(k)] = q
            q = q * tmass[k:k + 1, :]
            acc = q if acc is None else acc + q
        vec[4, pl.ds(a, 1), :] = jnp.sum(acc.T, axis=0, keepdims=True)

    def row_step(v):
        for a in range(BLK):
            acc = None
            for k in range(BLK):
                q = score[a, :, lanes(k)] * v[k:k + 1, :]
                acc = q if acc is None else acc + q
            vec[4, pl.ds(a, 1), :] = jnp.sum(acc.T, axis=0, keepdims=True)

    def col_step(u):
        acc = [jnp.zeros((8, LANES), jnp.float32)] * BLK
        for a in range(BLK):
            uc = col_form(u[a:a + 1, :])
            for k in range(BLK):
                acc[k] = acc[k] + jnp.sum(fold(score[a, :, lanes(k)] * uc), axis=0)
        for k in range(BLK):
            vec[5, pl.ds(k, 1), :] = jnp.sum(acc[k], axis=0, keepdims=True)

    def mate_scores():
        for kind in range(2):
            gather_end(kind)
            feats = gath[kind].reshape(TILE, LANES).astype(jnp.bfloat16)
            for part_at, xb in enumerate((x, mate_x[1 - kind])):
                d = lax.dot_general(xs[pl.ds(xb * 256, 256), :], feats, (((1,), (1,)), ((), ())),
                                    preferred_element_type=jnp.float32)
                pscore[kind, pl.ds(part_at * 256, 256), :] = d * (2.0 * norm_scale)

    def take(n):
        gather_end(2 + n)
        pteach[n] = gath[2 + n].reshape(TILE, LANES).astype(jnp.bfloat16)

    def mate_weights():
        for kind in range(2):
            arrive(kvec.at[1 + kind], kr_sem.at[kind])
            for b in range(4):
                xb = (x, mate_x[1 - kind])[b // 2]
                lc = col_form(vec[6, pl.ds(2 * xb + b % 2, 1), :])
                for k in range(BLK):
                    w = jnp.exp2(pscore[kind, pl.ds(b * LANES, LANES), lanes(k)] - lc + kvec[1 + kind, k:k + 1, :])
                    pweights[kind, pl.ds(b * LANES, LANES), lanes(k)] = w.astype(jnp.bfloat16)

    def during_col1():
        take(0)
        take(1)
        gather_share(0, 1)

    def during_row2():
        mate_scores()
        gather_share(4, 5)

    def during_col2():
        take(2)
        take(3)

    r = jnp.sum(row_exchange(1, vec[4], lambda: gather_share(2, 3)), axis=0)
    gather_send(4, 5)
    col_step(smass / r)
    cs = jnp.sum(col_exchange(1, vec[5], during_col1), axis=0)
    row_step(tmass / cs)
    r = jnp.sum(row_exchange(2, vec[4], during_row2), axis=0)
    gather_send(*range(6, 2 + NH))
    f_out[...] = (nx2 - row2) * (EPS * LN2) - EPS * jnp.log(r)
    col_step(smass / r)
    cs = jnp.sum(col_exchange(2, vec[5], during_col2), axis=0)
    kvec[0] = tlm2 - jnp.log(cs) * LOG2E - col2
    for kind in range(2):
        remote(kvec.at[0], kvec.at[1 + kind], ks_sem.at[kind], kr_sem.at[kind], mates[kind])
    gather_spread(*range(6, 2 + NH))
    g_out[...] = (ny2 - col2) * (EPS * LN2) - EPS * jnp.log(cs)

    v = tmass / cs
    for a in range(BLK):
        acc = None
        for k in range(BLK):
            q = (score[a, :, lanes(k)] * v[k:k + 1, :]).astype(jnp.bfloat16)
            weights[pl.ds(a * LANES, LANES), lanes(k)] = q
            q = q.astype(jnp.float32)
            acc = q if acc is None else acc + q
        tmp4[a // 2, pl.ds(a % 2, 1), :] = jnp.sum(acc.T, axis=0, keepdims=True)

    def project(ch):
        p = jnp.dot(weights[...], teach[:, ch * LANES:(ch + 2) * LANES], preferred_element_type=jnp.float32)
        part[ch] = p[:, :LANES].reshape(NX, NZ, ROWS, LANES)
        part[ch + 1] = p[:, LANES:].reshape(NX, NZ, ROWS, LANES)

    lo, hi = pl.ds(0, 4), pl.ds(4, 4)
    xr, xl = at_tgt(1, 0), at_tgt(-1, 0)
    zr, zl = at_tgt(0, 1), at_tgt(0, -1)

    def a_start(i, ch):
        remote(part.at[ch, xi[2], lo], xfar.at[i, 0], as_sem.at[i], ar_sem.at[i, 0], xr)
        remote(part.at[ch, xi[2], hi], xfar.at[i, 1], as_sem.at[i], ar_sem.at[i, 1], xl)

    def a_own(i, ch):
        remote(part.at[ch, xi[1], hi], xnear.at[i, 0, hi], as_sem.at[i], ar_sem.at[i, 2], xr)
        remote(part.at[ch, xi[3], lo], xnear.at[i, 1, lo], as_sem.at[i], ar_sem.at[i, 3], xl)

    def a_pass(i, ch, way):
        dev, dst, half = ((xr, xi[1], lo), (xl, xi[3], hi))[way]
        arrive(xfar.at[i, way], ar_sem.at[i, way])
        part[ch, dst, half] = part[ch, dst, half] + xfar[i, way]
        remote(part.at[ch, dst, half], xnear.at[i, way, half], as_sem.at[i], ar_sem.at[i, 2 + way], dev)

    def a_mid(i, ch):
        arrive(xnear.at[i, 0], ar_sem.at[i, 2])
        arrive(xnear.at[i, 1], ar_sem.at[i, 3])
        asum[i] = part[ch, x] + xnear[i, 0] + xnear[i, 1]
        z_start(i, ch)

    def a_ring(i, ch, step, way):
        dev, dst = ((zr, zi[4 - step]), (zl, zi[4 + step]))[way]
        if step == 1:
            arrive(zfar.at[i, way], zr_sem.at[i, way, 0])
            half = pl.ds(16 * way, 16)
            asum[i, dst, half] = asum[i, dst, half] + zfar[i, way]
        else:
            arrive(znear.at[i, way, step - 2], zr_sem.at[i, way, step - 1])
            asum[i, dst] = asum[i, dst] + znear[i, way, step - 2]
        remote(asum.at[i, dst], znear.at[i, way, step - 1], zs_sem.at[i], zr_sem.at[i, way, step], dev)

    def finish(ch, value):
        scale = rcol[lax.div(z, 4), pl.ds(lax.rem(z, 4) * ROWS, ROWS), :]
        out[:, lanes(ch)] = (value * scale).astype(jnp.bfloat16)

    def a_end(i, ch):
        arrive(znear.at[i, 0, 2], zr_sem.at[i, 0, 3])
        arrive(znear.at[i, 1, 2], zr_sem.at[i, 1, 3])
        finish(ch, asum[i, z] + znear[i, 0, 2] + znear[i, 1, 2])

    ends = (pl.ds(0, 2), pl.ds(2, 2))

    def b_start(i, ch):
        for way, dev in ((0, zr), (1, zl)):
            remote(part.at[ch, ends[way], zi[4]], bfar.at[i, way], bs_sem.at[i], br_sem.at[i, way, 0], dev)

    def b_own(i, ch):
        for way, dev, near in ((0, zr, zi[3]), (1, zl, zi[5])):
            own = 1 - way
            remote(part.at[ch, ends[own], near], bnear.at[i, way, 0, ends[own]], bs_sem.at[i], br_sem.at[i, way, 1], dev)

    def b_ring(i, ch, step, way):
        dev, dst = ((zr, zi[4 - step]), (zl, zi[4 + step]))[way]
        if step == 1:
            arrive(bfar.at[i, way], br_sem.at[i, way, 0])
            part[ch, ends[way], dst] = part[ch, ends[way], dst] + bfar[i, way]
            remote(part.at[ch, ends[way], dst], bnear.at[i, way, 0, ends[way]], bs_sem.at[i], br_sem.at[i, way, 1], dev)
        else:
            arrive(bnear.at[i, way, step - 2], br_sem.at[i, way, step - 1])
            part[ch, :, dst] = part[ch, :, dst] + bnear[i, way, step - 2]
            remote(part.at[ch, :, dst], bnear.at[i, way, step - 1], bs_sem.at[i], br_sem.at[i, way, step], dev)

    def b_mid(i, ch):
        arrive(bnear.at[i, 0, 2], br_sem.at[i, 0, 3])
        arrive(bnear.at[i, 1, 2], br_sem.at[i, 1, 3])
        bsum[i] = part[ch, :, z] + bnear[i, 0, 2] + bnear[i, 1, 2]
        for d in (2, 1, 3):
            remote(bsum.at[i, xi[d]], bx.at[i, d - 1], bxs_sem.at[i], bxr_sem.at[i], at_tgt(d, 0))

    def b_end(i, ch):
        arrive(bx.at[i], bxr_sem.at[i])
        finish(ch, bsum[i, x] + bx[i, 0] + bx[i, 1] + bx[i, 2])

    def h_start(n, ch):
        kind = n % 2
        for part_at, xb in enumerate((x, mate_x[1 - kind])):
            p = jnp.dot(weights[pl.ds(xb * 256, 256), :], teach[:, lanes(ch)], preferred_element_type=jnp.float32)
            p = p + jnp.dot(pweights[kind, pl.ds(part_at * 256, 256), :], pteach[n], preferred_element_type=jnp.float32)
            if part_at == 0:
                asum[NA + n] = p.reshape(NZ, ROWS, LANES)
            else:
                hsend[n] = p.reshape(NZ, ROWS, LANES)
        remote(hsend.at[n], hrecv.at[n], hs_sem.at[n], hr_sem.at[n], mates[1 - kind])

    def z_start(i, ch):
        if ch in DIRECT:
            for d in (4, 3, 5, 2, 6, 1, 7):
                remote(asum.at[i, zi[d]], zall.at[DIRECT.index(ch), d - 1], zs_sem.at[i], zr_sem.at[i, 0, 0], at_tgt(0, d))
        else:
            remote(asum.at[i, zi[4], pl.ds(0, 16)], zfar.at[i, 0], zs_sem.at[i], zr_sem.at[i, 0, 0], zr)
            remote(asum.at[i, zi[4], pl.ds(16, 16)], zfar.at[i, 1], zs_sem.at[i], zr_sem.at[i, 1, 0], zl)

    def a_direct(i, ch):
        n = DIRECT.index(ch)
        arrive(zall.at[n], zr_sem.at[i, 0, 0])
        total = asum[i, z]
        for d in range(7):
            total = total + zall[n, d]
        finish(ch, total)

    def h_mid(n, ch):
        arrive(hrecv.at[n], hr_sem.at[n])
        asum[NA + n] = asum[NA + n] + hrecv[n]
        z_start(NA + n, ch)

    def q_start():
        for d in (2, 1, 3):
            remote(tmp4.at[xi[d]], qbuf.at[d - 1], qs_sem.at[0], qr_sem.at[0], at_tgt(d, 0))

    def q_mid():
        arrive(qbuf.at[pl.ds(0, 3)], qr_sem.at[0])
        tmp4[x] = tmp4[x] + qbuf[0] + qbuf[1] + qbuf[2]
        for d in (4, 3, 5, 2, 6, 1, 7):
            remote(tmp4.at[x], qbuf.at[2 + d], qs_sem.at[1], qr_sem.at[1], at_tgt(0, d))

    def q_end():
        arrive(qbuf.at[pl.ds(3, 7)], qr_sem.at[1])
        total = tmp4[x]
        for d in range(7):
            total = total + qbuf[3 + d]
        rcol[0] = col_form(1.0 / total[0:1, :])
        rcol[1] = col_form(1.0 / total[1:2, :])

    steps = dict(ad=a_direct, hm=h_mid, ap=a_pass, am=a_mid, ar=a_ring, ae=a_end, br=b_ring, bm=b_mid, be=b_end)
    ready = set()
    q_start()
    for name, ch, *rest in SCHEDULE:
        if name == "qm":
            q_mid()
        elif name == "qe":
            q_end()
        elif name == "hw":
            mate_weights()
        elif name == "hf":
            gather_share(6 + 2 * ch, 7 + 2 * ch)
        elif name == "ht":
            take(4 + 2 * ch)
            take(5 + 2 * ch)
        elif name == "ao":
            a_own(KINDS[:ch].count("A"), ch)
        elif name == "bo":
            b_own(KINDS[:ch].count("B"), ch)
        elif name == "s" and KINDS[ch] == "H":
            h_start(KINDS[:ch].count("H"), ch)
        elif name == "s":
            if ch // 2 not in ready:
                ready.add(ch // 2)
                project(ch // 2 * 2)
            (a_start if KINDS[ch] == "A" else b_start)(KINDS[:ch].count(KINDS[ch]), ch)
        elif KINDS[ch] == "H" and name in ("ar", "ae", "ad"):
            steps[name](NA + KINDS[:ch].count("H"), ch, *rest)
        else:
            steps[name](KINDS[:ch].count(KINDS[ch]), ch, *rest)

    for e in range(3):
        arrive(rbuf.at[e, pl.ds(0, 31)], rs_sem.at[e])
        arrive(cbuf.at[e, pl.ds(0, 7)], cs_sem.at[e])
    arrive(qbuf.at[pl.ds(0, 3)], qs_sem.at[0])
    arrive(qbuf.at[pl.ds(3, 7)], qs_sem.at[1])
    for i, ch in enumerate(chunks_of("A")):
        arrive(part.at[ch, pl.ds(0, 3)], as_sem.at[i])
    for i in range(NA + NH):
        arrive(asum.at[i, pl.ds(0, 7)], zs_sem.at[i])
    for n in range(NH):
        arrive(hsend.at[n], hs_sem.at[n])
    for u in range(2 + NH):
        if shared(u):
            arrive(stage.at[u, 0], gs_sem.at[u])
            arrive(gath.at[u, 0, pl.ds(0, 3)], ys_sem.at[u])
        else:
            arrive(stage.at[u], gs_sem.at[u])
        arrive(stage.at[u], ds_sem.at[u])
    for kind in range(2):
        arrive(kvec.at[0], ks_sem.at[kind])
    for i, ch in enumerate(chunks_of("B")):
        arrive(part.at[ch, :, pl.ds(0, 7)], bs_sem.at[i])
        arrive(bx.at[i], bxs_sem.at[i])


def settle(*refs):
    sem = refs[-1]
    copies = [pltpu.make_async_copy(refs[n], refs[3 + n], sem.at[n]) for n in range(3)]
    for copy in copies:
        copy.start()
    for copy in copies:
        copy.wait()


def body(source_features, target_features, source_logmass, target_logmass, teacher_rows):
    na, nb, nz = NA, KINDS.count("B"), NA + NH
    f32 = jnp.float32
    vmem = pl.BlockSpec(memory_space=pltpu.VMEM)
    dma = pltpu.SemaphoreType.DMA
    projected, f, g = pl.pallas_call(
        functools.partial(kernel, source_features.shape[1]),
        out_shape=(
            jax.ShapeDtypeStruct((ROWS, CHUNKS * LANES), jnp.bfloat16),
            jax.ShapeDtypeStruct((BLK, LANES), f32),
            jax.ShapeDtypeStruct((BLK, LANES), f32),
        ),
        in_specs=[pl.BlockSpec(memory_space=pltpu.HBM)] * 5,
        out_specs=(vmem, vmem, vmem),
        scratch_shapes=[
            pltpu.VMEM(source_features.shape, source_features.dtype),
            pltpu.VMEM(target_features.shape, target_features.dtype),
            pltpu.VMEM((BLK, LANES), f32),
            pltpu.VMEM((BLK, LANES), f32),
            pltpu.VMEM((BLK, LANES, TILE), f32),
            pltpu.VMEM((BLK, LANES, LANES), f32),
            pltpu.VMEM((TILE, TILE), jnp.bfloat16),
            pltpu.VMEM((TILE, CHUNKS * LANES), jnp.bfloat16),
            pltpu.VMEM((CHUNKS, NX, NZ, ROWS, LANES), f32),
            pltpu.VMEM((3, 32, BLK, LANES), f32),
            pltpu.VMEM((3, 8, BLK, LANES), f32),
            pltpu.VMEM((7, BLK, LANES), f32),
            pltpu.VMEM((NX, 2, LANES), f32),
            pltpu.VMEM((10, 2, LANES), f32),
            pltpu.VMEM((na, 2, 4, ROWS, LANES), f32),
            pltpu.VMEM((na, 2, NZ, ROWS, LANES), f32),
            pltpu.VMEM((nz, NZ, ROWS, LANES), f32),
            pltpu.VMEM((nz, 2, ROWS // 2, LANES), f32),
            pltpu.VMEM((nz, 2, 3, ROWS, LANES), f32),
            pltpu.VMEM((nb, 2, 2, ROWS, LANES), f32),
            pltpu.VMEM((nb, 2, 3, NX, ROWS, LANES), f32),
            pltpu.VMEM((nb, NX, ROWS, LANES), f32),
            pltpu.VMEM((nb, 3, ROWS, LANES), f32),
            pltpu.VMEM((2, LANES, LANES), f32),
            dma, dma((4,)), dma((3,)), dma((3,)), dma((3,)), dma((3,)), dma((2,)), dma((2,)),
            dma((na,)), dma((na, 4)), dma((nz,)), dma((nz, 2, 4)),
            dma((nb,)), dma((nb, 2, 4)), dma((nb,)), dma((nb,)),
            pltpu.VMEM((max(1, len(DIRECT)), 7, ROWS, LANES), f32),
            pltpu.VMEM((2 + NH, 4, LANES, LANES), f32),
            pltpu.VMEM((2 + NH, 2, 4, LANES, LANES), f32),
            pltpu.VMEM((2, HALF, TILE), f32),
            pltpu.VMEM((2, HALF, TILE), jnp.bfloat16),
            pltpu.VMEM((NH, TILE, LANES), jnp.bfloat16),
            pltpu.VMEM((3, BLK, LANES), f32),
            pltpu.VMEM((NH, NZ, ROWS, LANES), f32),
            pltpu.VMEM((NH, NZ, ROWS, LANES), f32),
            dma((2 + NH,)), dma((2 + NH,)), dma((2 + NH,)), dma((2 + NH,)), dma((2 + NH,)), dma((2 + NH,)), dma((2,)), dma((2,)), dma((NH,)), dma((NH,)),
        ],
        compiler_params=pltpu.CompilerParams(
            collective_id=0, has_side_effects=True, vmem_limit_bytes=(64 * 1024 - 192) * 1024),
    )(source_features, target_features, source_logmass.reshape(BLK, LANES),
      target_logmass.reshape(BLK, LANES), teacher_rows)
    return pl.pallas_call(
        settle,
        out_shape=(
            jax.ShapeDtypeStruct(projected.shape, jnp.bfloat16),
            jax.ShapeDtypeStruct((TILE,), f32),
            jax.ShapeDtypeStruct((TILE,), f32),
        ),
        in_specs=[vmem] * 3,
        out_specs=(pl.BlockSpec(memory_space=pl.ANY),) * 3,
        scratch_shapes=[dma((3,))],
    )(projected, f.reshape(TILE), g.reshape(TILE))


def solution(mesh):
    in_specs = (P("src", None), P("tgt", None), P("src"), P("tgt"), P("tgt", None))
    out_specs = (P(("src", "tgt"), None), P("src"), P("tgt"))
    return jax.shard_map(body, mesh=mesh, in_specs=in_specs, out_specs=out_specs, check_vma=False)
```

profile of v0, /device:TPU:8, one launch (start us, length us, event | category | flops | bytes accessed | tf_op | source)
XLA Modules:
  0.0 85.4 jit_solution(4878337741463662246)
XLA Ops:
  0.6 83.0 %shard_map.76 = (bf16[32,1536]{1,0:T(8,128)(2,1)}, f32[8,128]{1,0:T(8,128)}, f32[8,128]{1,0:T(8,128)}) custom-call(bf16[1024,128]{1,0:T(8,128)(2,1)} %xs_hbm.1, bf16[1024,128]{1,0:T(8,128)(2,1)} %ys_hbm.1, f32[8,128]{1,0:T(8,128)} %bitcast.4, f32[8,128]{1,0:T(8,128)} %bitcast.5, bf16[1024,1536]{1,0:T(8,128)(2,1)} %rows_hbm.1), custom_call_target="tpu_custom_call" | custom-call | tf_op jit(solution)/shard_map/pallas_call | solution.py:507
  83.7 1.6 %shard_map.77 = (bf16[32,1536]{1,0:T(8,128)(2,1)}, f32[1024]{0:T(1024)}, f32[1024]{0:T(1024)}) custom-call(bf16[32,1536]{1,0:T(8,128)(2,1)} %get-tuple-element.6.refs_0_, f32[1024]{0:T(1024)} %bitcast.6, f32[1024]{0:T(1024)} %bitcast.7), custom_call_target="tpu_custom_call" | custom-call | tf_op jit(solution)/shard_map/pallas_call | solution.py:559
where the time goes:
time: 85.5 us; the launch traced here: 85.4 us
  Pallas kernels  84.6 us (99%)
    pallas_call x1, Pallas kernels, body(): pl.pallas_call(functools.partial(kernel, source_features.shape[1]), out_s...  83 us

commit v1 on v0

--- a/solution.py
+++ b/solution.py
@@ -20,25 +20,25 @@
 HALF = TILE // 2
 NEAR = 4
 CHUNKS = 12
-KINDS = "ABABBAHHHHHH"
-DIRECT = (1, 3, 5)
+KINDS = "ABBABAHHHHHH"
+DIRECT = (2, 4, 5)
 SCHEDULE = (
-    ("s", 0), ("s", 1), ("ao", 0), ("bo", 1), ("s", 2), ("s", 3), ("qm", 0), ("s", 4), ("br", 1, 1, 0),
-    ("br", 1, 1, 1), ("ao", 2), ("bo", 3), ("ap", 0, 0), ("ap", 0, 1), ("bo", 4), ("hw", 0), ("s", 6), ("hf", 0),
-    ("br", 3, 1, 0), ("br", 3, 1, 1), ("s", 7), ("br", 4, 1, 0), ("ap", 2, 0), ("ap", 2, 1), ("br", 4, 1, 1),
-    ("br", 1, 2, 0), ("br", 1, 2, 1), ("s", 8), ("s", 9), ("ht", 0), ("s", 10), ("br", 3, 2, 0), ("br", 3, 2, 1),
-    ("am", 0), ("br", 4, 2, 0), ("br", 4, 2, 1), ("s", 11), ("br", 1, 3, 0), ("br", 1, 3, 1), ("hm", 7), ("hm", 6),
-    ("br", 3, 3, 0), ("br", 3, 3, 1), ("ar", 0, 1, 0), ("ar", 0, 1, 1), ("am", 2), ("br", 4, 3, 0), ("br", 4, 3, 1),
-    ("s", 5), ("ao", 5), ("bm", 1), ("ar", 7, 1, 0), ("ar", 7, 1, 1), ("ar", 6, 1, 0), ("ar", 6, 1, 1), ("hm", 8),
-    ("hm", 9), ("bm", 3), ("ar", 0, 2, 0), ("ar", 0, 2, 1), ("ar", 2, 1, 0), ("ar", 2, 1, 1), ("hm", 11), ("hm", 10),
-    ("bm", 4), ("ar", 7, 2, 0), ("ar", 7, 2, 1), ("ar", 6, 2, 0), ("ar", 6, 2, 1), ("ar", 8, 1, 0), ("ar", 8, 1, 1),
-    ("ar", 9, 1, 0), ("ar", 9, 1, 1), ("ap", 5, 0), ("ar", 0, 3, 0), ("ar", 0, 3, 1), ("ap", 5, 1), ("ar", 2, 2, 0),
-    ("ar", 2, 2, 1), ("ar", 11, 1, 0), ("ar", 11, 1, 1), ("ar", 10, 1, 0), ("ar", 10, 1, 1), ("qe", 0), ("be", 1),
-    ("ar", 7, 3, 0), ("ar", 7, 3, 1), ("ar", 6, 3, 0), ("ar", 6, 3, 1), ("be", 3), ("ar", 8, 2, 0), ("ar", 8, 2, 1),
-    ("ar", 9, 2, 0), ("ar", 9, 2, 1), ("be", 4), ("ae", 0), ("ar", 2, 3, 0), ("ar", 2, 3, 1), ("ar", 11, 2, 0),
-    ("ar", 11, 2, 1), ("ar", 10, 2, 0), ("ar", 10, 2, 1), ("am", 5), ("ae", 7), ("ae", 6), ("ar", 8, 3, 0),
-    ("ar", 8, 3, 1), ("ar", 9, 3, 0), ("ar", 9, 3, 1), ("ae", 2), ("ar", 11, 3, 0), ("ar", 11, 3, 1),
-    ("ar", 10, 3, 0), ("ar", 10, 3, 1), ("ad", 5), ("ae", 8), ("ae", 9), ("ae", 11), ("ae", 10),
+    ("s", 0), ("s", 1), ("s", 2), ("ao", 0), ("bo", 1), ("bo", 2), ("s", 3), ("qm", 0), ("s", 4), ("ao", 3),
+    ("bo", 4), ("br", 1, 1, 0), ("br", 1, 1, 1), ("hw", 0), ("s", 6), ("br", 2, 1, 0), ("br", 2, 1, 1), ("ap", 0, 0),
+    ("ap", 0, 1), ("hf", 0), ("br", 4, 1, 0), ("br", 4, 1, 1), ("s", 7), ("ap", 3, 0), ("ap", 3, 1), ("br", 1, 2, 0),
+    ("br", 1, 2, 1), ("s", 8), ("br", 2, 2, 0), ("br", 2, 2, 1), ("br", 4, 2, 0), ("br", 4, 2, 1), ("s", 9),
+    ("hm", 6), ("br", 1, 3, 0), ("br", 1, 3, 1), ("ht", 0), ("s", 10), ("hm", 7), ("br", 2, 3, 0), ("br", 2, 3, 1),
+    ("am", 0), ("s", 11), ("am", 3), ("br", 4, 3, 0), ("br", 4, 3, 1), ("ar", 6, 1, 0), ("ar", 6, 1, 1), ("s", 5),
+    ("ao", 5), ("bm", 1), ("ar", 7, 1, 0), ("hm", 9), ("hm", 8), ("ar", 7, 1, 1), ("bm", 2), ("ar", 0, 1, 0),
+    ("ar", 0, 1, 1), ("ar", 3, 1, 0), ("ar", 3, 1, 1), ("hm", 11), ("bm", 4), ("hm", 10), ("ar", 6, 2, 0),
+    ("ar", 6, 2, 1), ("ar", 9, 1, 0), ("ar", 9, 1, 1), ("ar", 8, 1, 0), ("ar", 8, 1, 1), ("ap", 5, 0), ("ap", 5, 1),
+    ("ar", 7, 2, 0), ("ar", 7, 2, 1), ("ar", 0, 2, 0), ("ar", 0, 2, 1), ("ar", 3, 2, 0), ("ar", 3, 2, 1),
+    ("ar", 11, 1, 0), ("ar", 11, 1, 1), ("ar", 10, 1, 0), ("ar", 10, 1, 1), ("ar", 6, 3, 0), ("qe", 0), ("be", 1),
+    ("ar", 6, 3, 1), ("ar", 9, 2, 0), ("ar", 9, 2, 1), ("ar", 8, 2, 0), ("be", 2), ("ar", 8, 2, 1), ("ar", 7, 3, 0),
+    ("ar", 7, 3, 1), ("ar", 0, 3, 0), ("be", 4), ("ar", 0, 3, 1), ("ar", 3, 3, 0), ("ar", 3, 3, 1), ("ar", 11, 2, 0),
+    ("ar", 11, 2, 1), ("ar", 10, 2, 0), ("ar", 10, 2, 1), ("am", 5), ("ae", 6), ("ar", 9, 3, 0), ("ar", 9, 3, 1),
+    ("ar", 8, 3, 0), ("ar", 8, 3, 1), ("ae", 7), ("ae", 0), ("ae", 3), ("ar", 11, 3, 0), ("ar", 11, 3, 1),
+    ("ar", 10, 3, 0), ("ar", 10, 3, 1), ("ad", 5), ("ae", 9), ("ae", 8), ("ae", 11), ("ae", 10),
 )
 NA, NH = KINDS.count("A"), KINDS.count("H")
 
@@ -182,13 +182,15 @@
         s = jnp.sum(s, axis=1, keepdims=True)
         lse = m + jnp.log(s) * LOG2E
         vec[2, pl.ds(a, 1), :] = jnp.broadcast_to(lse, (LANES, LANES)).T[0:1, :]
-    stage[0] = ys[mine, :].astype(jnp.float32).reshape(4, LANES, LANES)
-    stage[1] = stage[0]
-    load.wait()
-    for n, ch in enumerate(chunks_of("H")):
-        stage[2 + n] = teach[mine, lanes(ch)].astype(jnp.float32).reshape(4, LANES, LANES)
+    def fill_stage():
+        stage[0] = ys[mine, :].astype(jnp.float32).reshape(4, LANES, LANES)
+        stage[1] = stage[0]
+        load.wait()
+        for n, ch in enumerate(chunks_of("H")):
+            stage[2 + n] = teach[mine, lanes(ch)].astype(jnp.float32).reshape(4, LANES, LANES)
+
     pl.semaphore_wait(barrier, len(tgt_peers) + len(src_peers))
-    row2 = lse2(row_exchange(0, vec[2]))
+    row2 = lse2(row_exchange(0, vec[2], fill_stage))
     vec[6] = row2
     gather_send(0, 1, 2, 3)
 

time: 85.5 us -> 84.7 us (level)
  Pallas kernels: 84.6 us -> 83.5 us
    pallas_call x1, Pallas kernels: 83 us -> 81.9 us  [body(): pl.pallas_call(functools.partial(kernel, source_features.shape[1]), out_s...]
where the time goes in v1:
time: 84.7 us; the launch traced here: 84.3 us
  Pallas kernels  83.5 us (99%)
    pallas_call x1, Pallas kernels, body(): pl.pallas_call(functools.partial(kernel, source_features.shape[1]), out_s...  81.9 us

profile of v1, /device:TPU:8, one launch (start us, length us, event | category | flops | bytes accessed | tf_op | source)
XLA Modules:
  0.0 84.3 jit_solution(973527234675597651)
XLA Ops:
  0.6 81.9 %shard_map.76 = (bf16[32,1536]{1,0:T(8,128)(2,1)}, f32[8,128]{1,0:T(8,128)}, f32[8,128]{1,0:T(8,128)}) custom-call(bf16[1024,128]{1,0:T(8,128)(2,1)} %xs_hbm.1, bf16[1024,128]{1,0:T(8,128)(2,1)} %ys_hbm.1, f32[8,128]{1,0:T(8,128)} %bitcast.4, f32[8,128]{1,0:T(8,128)} %bitcast.5, bf16[1024,1536]{1,0:T(8,128)(2,1)} %rows_hbm.1), custom_call_target="tpu_custom_call" | custom-call | tf_op jit(solution)/shard_map/pallas_call | solution.py:509
  82.6 1.6 %shard_map.77 = (bf16[32,1536]{1,0:T(8,128)(2,1)}, f32[1024]{0:T(1024)}, f32[1024]{0:T(1024)}) custom-call(bf16[32,1536]{1,0:T(8,128)(2,1)} %get-tuple-element.6.refs_0_, f32[1024]{0:T(1024)} %bitcast.6, f32[1024]{0:T(1024)} %bitcast.7), custom_call_target="tpu_custom_call" | custom-call | tf_op jit(solution)/shard_map/pallas_call | solution.py:561

commit v2 on v1

--- a/solution.py
+++ b/solution.py
@@ -211,6 +211,9 @@
         total = jnp.sum(sums[k], axis=0, keepdims=True)
         vec[3, pl.ds(k, 1), :] = peaks[k] + jnp.log(total) * LOG2E
     col2 = lse2(col_exchange(0, vec[3]))
+    kvec[3] = col2
+    for kind in range(2):
+        remote(kvec.at[3], kvec.at[4 + kind], ks_sem.at[2 + kind], kr_sem.at[2 + kind], mates[kind])
     gather_spread(0, 1)
 
     tmass = jnp.exp(tlm[...])
@@ -250,6 +253,13 @@
                 d = lax.dot_general(xs[pl.ds(xb * 256, 256), :], feats, (((1,), (1,)), ((), ())),
                                     preferred_element_type=jnp.float32)
                 pscore[kind, pl.ds(part_at * 256, 256), :] = d * (2.0 * norm_scale)
+            arrive(kvec.at[4 + kind], kr_sem.at[2 + kind])
+            for b in range(4):
+                xb = (x, mate_x[1 - kind])[b // 2]
+                lc = col_form(vec[6, pl.ds(2 * xb + b % 2, 1), :])
+                for k in range(BLK):
+                    at = (kind, pl.ds(b * LANES, LANES), lanes(k))
+                    pscore[at] = jnp.exp2(pscore[at] - lc - kvec[4 + kind, k:k + 1, :])
 
     def take(n):
         gather_end(2 + n)
@@ -259,10 +269,8 @@
         for kind in range(2):
             arrive(kvec.at[1 + kind], kr_sem.at[kind])
             for b in range(4):
-                xb = (x, mate_x[1 - kind])[b // 2]
-                lc = col_form(vec[6, pl.ds(2 * xb + b % 2, 1), :])
                 for k in range(BLK):
-                    w = jnp.exp2(pscore[kind, pl.ds(b * LANES, LANES), lanes(k)] - lc + kvec[1 + kind, k:k + 1, :])
+                    w = pscore[kind, pl.ds(b * LANES, LANES), lanes(k)] * kvec[1 + kind, k:k + 1, :]
                     pweights[kind, pl.ds(b * LANES, LANES), lanes(k)] = w.astype(jnp.bfloat16)
 
     def during_col1():
@@ -288,7 +296,7 @@
     f_out[...] = (nx2 - row2) * (EPS * LN2) - EPS * jnp.log(r)
     col_step(smass / r)
     cs = jnp.sum(col_exchange(2, vec[5], during_col2), axis=0)
-    kvec[0] = tlm2 - jnp.log(cs) * LOG2E - col2
+    kvec[0] = tmass / cs
     for kind in range(2):
         remote(kvec.at[0], kvec.at[1 + kind], ks_sem.at[kind], kr_sem.at[kind], mates[kind])
     gather_spread(*range(6, 2 + NH))
@@ -485,7 +493,7 @@
         else:
             arrive(stage.at[u], gs_sem.at[u])
         arrive(stage.at[u], ds_sem.at[u])
-    for kind in range(2):
+    for kind in range(4):
         arrive(kvec.at[0], ks_sem.at[kind])
     for i, ch in enumerate(chunks_of("B")):
         arrive(part.at[ch, :, pl.ds(0, 7)], bs_sem.at[i])
@@ -549,10 +557,10 @@
             pltpu.VMEM((2, HALF, TILE), f32),
             pltpu.VMEM((2, HALF, TILE), jnp.bfloat16),
             pltpu.VMEM((NH, TILE, LANES), jnp.bfloat16),
-            pltpu.VMEM((3, BLK, LANES), f32),
+            pltpu.VMEM((6, BLK, LANES), f32),
             pltpu.VMEM((NH, NZ, ROWS, LANES), f32),
             pltpu.VMEM((NH, NZ, ROWS, LANES), f32),
-            dma((2 + NH,)), dma((2 + NH,)), dma((2 + NH,)), dma((2 + NH,)), dma((2 + NH,)), dma((2 + NH,)), dma((2,)), dma((2,)), dma((NH,)), dma((NH,)),
+            dma((2 + NH,)), dma((2 + NH,)), dma((2 + NH,)), dma((2 + NH,)), dma((2 + NH,)), dma((2 + NH,)), dma((4,)), dma((4,)), dma((NH,)), dma((NH,)),
         ],
         compiler_params=pltpu.CompilerParams(
             collective_id=0, has_side_effects=True, vmem_limit_bytes=(64 * 1024 - 192) * 1024),

time: 84.7 us -> 84.5 us (level)
  no operation moved by 1% of the time
where the time goes in v2:
time: 84.5 us; the launch traced here: 84.2 us
  Pallas kernels  83.4 us (99%)
    pallas_call x1, Pallas kernels, body(): pl.pallas_call(functools.partial(kernel, source_features.shape[1]), out_s...  81.9 us

profile of v2, /device:TPU:8, one launch (start us, length us, event | category | flops | bytes accessed | tf_op | source)
XLA Modules:
  0.0 84.2 jit_solution(14853115551281157893)
XLA Ops:
  0.6 81.9 %shard_map.76 = (bf16[32,1536]{1,0:T(8,128)(2,1)}, f32[8,128]{1,0:T(8,128)}, f32[8,128]{1,0:T(8,128)}) custom-call(bf16[1024,128]{1,0:T(8,128)(2,1)} %xs_hbm.1, bf16[1024,128]{1,0:T(8,128)(2,1)} %ys_hbm.1, f32[8,128]{1,0:T(8,128)} %bitcast.4, f32[8,128]{1,0:T(8,128)} %bitcast.5, bf16[1024,1536]{1,0:T(8,128)(2,1)} %rows_hbm.1), custom_call_target="tpu_custom_call" | custom-call | tf_op jit(solution)/shard_map/pallas_call | solution.py:517
  82.5 1.6 %shard_map.77 = (bf16[32,1536]{1,0:T(8,128)(2,1)}, f32[1024]{0:T(1024)}, f32[1024]{0:T(1024)}) custom-call(bf16[32,1536]{1,0:T(8,128)(2,1)} %get-tuple-element.6.refs_0_, f32[1024]{0:T(1024)} %bitcast.6, f32[1024]{0:T(1024)} %bitcast.7), custom_call_target="tpu_custom_call" | custom-call | tf_op jit(solution)/shard_map/pallas_call | solution.py:569

commit v3 on v2

--- a/solution.py
+++ b/solution.py
@@ -317,6 +317,10 @@
         part[ch] = p[:, :LANES].reshape(NX, NZ, ROWS, LANES)
         part[ch + 1] = p[:, LANES:].reshape(NX, NZ, ROWS, LANES)
 
+    def project_one(ch):
+        p = jnp.dot(weights[...], teach[:, lanes(ch)], preferred_element_type=jnp.float32)
+        part[ch] = p.reshape(NX, NZ, ROWS, LANES)
+
     lo, hi = pl.ds(0, 4), pl.ds(4, 4)
     xr, xl = at_tgt(1, 0), at_tgt(-1, 0)
     zr, zl = at_tgt(0, 1), at_tgt(0, -1)
@@ -466,7 +470,9 @@
         elif name == "s" and KINDS[ch] == "H":
             h_start(KINDS[:ch].count("H"), ch)
         elif name == "s":
-            if ch // 2 not in ready:
+            if ch < 2:
+                project_one(ch)
+            elif ch // 2 not in ready:
                 ready.add(ch // 2)
                 project(ch // 2 * 2)
             (a_start if KINDS[ch] == "A" else b_start)(KINDS[:ch].count(KINDS[ch]), ch)

time: 84.5 us -> 86.2 us (1.020)
  Pallas kernels: 83.4 us -> 85.3 us
    pallas_call x1, Pallas kernels: 81.9 us -> 83.7 us  [body(): pl.pallas_call(functools.partial(kernel, source_features.shape[1]), out_s...]
where the time goes in v3:
time: 86.2 us; the launch traced here: 86.1 us
  Pallas kernels  85.3 us (99%)
    pallas_call x1, Pallas kernels, body(): pl.pallas_call(functools.partial(kernel, source_features.shape[1]), out_s...  83.7 us

profile of v3, /device:TPU:8, one launch (start us, length us, event | category | flops | bytes accessed | tf_op | source)
XLA Modules:
  0.0 86.1 jit_solution(17336401721275321497)
XLA Ops:
  0.6 83.7 %shard_map.76 = (bf16[32,1536]{1,0:T(8,128)(2,1)}, f32[8,128]{1,0:T(8,128)}, f32[8,128]{1,0:T(8,128)}) custom-call(bf16[1024,128]{1,0:T(8,128)(2,1)} %xs_hbm.1, bf16[1024,128]{1,0:T(8,128)(2,1)} %ys_hbm.1, f32[8,128]{1,0:T(8,128)} %bitcast.4, f32[8,128]{1,0:T(8,128)} %bitcast.5, bf16[1024,1536]{1,0:T(8,128)(2,1)} %rows_hbm.1), custom_call_target="tpu_custom_call" | custom-call | tf_op jit(solution)/shard_map/pallas_call | solution.py:523
  84.4 1.6 %shard_map.77 = (bf16[32,1536]{1,0:T(8,128)(2,1)}, f32[1024]{0:T(1024)}, f32[1024]{0:T(1024)}) custom-call(bf16[32,1536]{1,0:T(8,128)(2,1)} %get-tuple-element.6.refs_0_, f32[1024]{0:T(1024)} %bitcast.6, f32[1024]{0:T(1024)} %bitcast.7), custom_call_target="tpu_custom_call" | custom-call | tf_op jit(solution)/shard_map/pallas_call | solution.py:575
